TPU v7x, 256 devices: a whole 4x4x8 slice. The times are simulated.
256 devices in a mesh: job: 32 (over x, y, core), seq: 8 (over z).
Axes of the slice: x: 4, y: 4, z: 8, core: 2. Of those that a mesh axis runs over, the one named last changes fastest.
Arguments:
- text_cache: bfloat16 [32, 2, 512, 4096], P('job', None, 'seq'), may hold values from -6 to 6
- source: int32 [32], replicated, may hold values from 0 to 63, as said below
- text_len: int32 [32], replicated, may hold values from 1 to 512, as said below
- query: bfloat16 [32, 2048, 3072], P('job', 'seq'), may hold values from -64 to 64
- w_text: bfloat16 [4096, 5120], P('job', 'seq'), may hold values from -0.09375 to 0.09375
- b_text: bfloat16 [5120], P('seq'), may hold values from -3 to 3
- w_key: bfloat16 [5120, 3072], P('job', 'seq'), may hold values from -0.078125 to 0.078125
- w_value: bfloat16 [5120, 3072], P('job', 'seq'), may hold values from -0.078125 to 0.078125
- b_value: bfloat16 [3072], P('seq'), may hold values from -3 to 3
Outputs:
- attended: bfloat16 [32, 2048, 3072], P('job', 'seq')
Inputs may be any that keep to these rules, and one draw needn't show every extreme that they name: `source`: entries are distinct flat cache indices; 0 and 63 occur in every draw. `text_len`: some group has 512 live text tokens and some has 1.
All inputs are finite; a program needn't handle non-finite values.
Results may differ from a plain program's by a relative error of at most 0.008.
Values may be sent and summed in bfloat16 or wider, within the bound.
A program may use at most 128 MiB of HBM per device.

v0:
```python
import jax
import jax.numpy as jnp
from jax import lax
from jax.sharding import PartitionSpec as P

HD = 128


def attend(queries, keys, values, key_live):
    score_scale = HD ** (-0.5)
    scores = (
        jnp.einsum("rhd,khd->hrk", queries, keys, preferred_element_type=jnp.float32) * score_scale
    )
    scores = jnp.where(key_live[None, None, :], scores, jnp.float32(-1e30))
    row_peak = jnp.max(scores, axis=-1, keepdims=True)
    exponent = jnp.exp(scores - row_peak)
    probabilities = (exponent / jnp.sum(exponent, axis=-1, keepdims=True)).astype(jnp.bfloat16)
    mixed = jnp.einsum("hrk,khd->rhd", probabilities, values, preferred_element_type=jnp.float32)
    return mixed.astype(jnp.bfloat16).reshape(queries.shape[0], -1)


def add_product(left, portion):
    return jnp.dot(left, portion, preferred_element_type=jnp.float32)


def body(text_cache, source, text_len, query, w_text, b_text, w_key, w_value, b_value):
    groups = lax.axis_size("job")
    group_index = lax.axis_index("job")
    cached = text_cache[0]
    slot_count, rows_local, text_width = cached.shape
    portion_rows = rows_local // groups
    spread = lax.all_to_all(
        cached.reshape(slot_count, groups, portion_rows, text_width),
        "job",
        split_axis=1,
        concat_axis=1,
        tiled=True,
    )
    holder = source // slot_count
    slot_of = source % slot_count
    picked = spread[slot_of, holder]
    arrived = lax.all_to_all(picked, "job", split_axis=0, concat_axis=0, tiled=True).reshape(
        rows_local, text_width
    )
    text_rows = lax.all_gather(arrived, "seq", axis=0, tiled=True)
    text_count = text_rows.shape[0]
    preact = add_product(text_rows, lax.all_gather(w_text, "job", axis=0, tiled=True))
    hidden_part = jax.nn.gelu(preact + b_text.astype(jnp.float32), approximate=True).astype(
        jnp.bfloat16
    )
    hidden = lax.all_gather(hidden_part, "seq", axis=1, tiled=True)

    def single_step(portion):
        return add_product(hidden, portion)

    key_sums = single_step(lax.all_gather(w_key, "job", axis=0, tiled=True))
    value_sums = single_step(lax.all_gather(w_value, "job", axis=0, tiled=True))
    keys = key_sums.astype(jnp.bfloat16)
    values = (value_sums + b_value.astype(jnp.float32)).astype(jnp.bfloat16)
    key_live = jnp.arange(text_count) < text_len[group_index]
    queries = query[0]
    video_local = queries.shape[0]
    all_keys, all_values = (
        lax.all_gather(keys, "seq", axis=1, tiled=True),
        lax.all_gather(values, "seq", axis=1, tiled=True),
    )
    result = attend(
        queries.reshape(video_local, -1, HD),
        all_keys.reshape(text_count, -1, HD),
        all_values.reshape(text_count, -1, HD),
        key_live,
    )
    return result[None]


def solution(mesh):
    in_specs = (
        P("job", None, "seq", None),
        P(),
        P(),
        P("job", "seq", None),
        P("job", "seq"),
        P("seq"),
        P("job", "seq"),
        P("job", "seq"),
        P("seq"),
    )
    out_specs = P("job", "seq", None)
    return jax.shard_map(body, mesh=mesh, in_specs=in_specs, out_specs=out_specs, check_vma=False)
```

profile of v0, /device:TPU:2, one launch (start us, length us, event | category | flops | bytes accessed | tf_op | source)
XLA Modules:
  0.0 443.3 jit_solution(1020585032217924011)
XLA Ops:
  6.5 2.3 copy.20
  8.9 2.1 copy.21
  10.9 7.6 %all-to-all-start = ((bf16[2,32,2,4096]{3,2,0,1:T(2,128)(2,1)}), bf16[2,32,2,4096]{3,2,0,1:T(2,128)(2,1)S(1)}, u32[]{:S(2)}, u32[]{:S(2)}) async-start(bf16[2,32,2,4096]{3,2,0,1:T(2,128)(2,1)} %copy.21), calls=%async_computation | async-start | bytes 2097152 | tf_op jit(solution)/shard_map/all_to_all | solution.py:32
  18.6 0.0 all-gather.8.cloned.1.call-start
  18.7 14.4 %all-to-all-done = bf16[2,32,2,4096]{3,2,0,1:T(2,128)(2,1)S(1)} async-done(((bf16[2,32,2,4096]{3,2,0,1:T(2,128)(2,1)}), bf16[2,32,2,4096]{3,2,0,1:T(2,128)(2,1)S(1)}, u32[]{:S(2)}, u32[]{:S(2)}) %all-to-all-start) | async-done | bytes 1048608 | tf_op jit(solution)/shard_map/all_to_all | solution.py:32
  33.0 1.6 gather_fusion
  34.6 15.9 %all_to_all.10 = bf16[32,2,4096]{2,1,0:T(2,128)(2,1)S(1)} all-to-all(bf16[32,2,4096]{2,1,0:T(2,128)(2,1)S(1)} %gather_fusion), channel_id=1, replica_groups=mesh['job'=32,'seq'=8] {'job'}, dimensions={0} | all-to-all | bytes 1048576 | tf_op jit(solution)/shard_map/all_to_all | solution.py:42
  50.6 1.0 reshape.17
  51.6 0.0 all-gather.10.cloned.1.call-start
  51.6 0.7 all-gather.10.cloned.1.call-update
  52.4 0.7 all-gather.18.cloned.1.call-update
  53.1 54.3 %all-gather.8.cloned.1.call-done = bf16[512,4096]{1,0:T(8,128)(2,1)} async-done(((bf16[64,4096]{1,0:T(8,128)(2,1)}), bf16[512,4096]{1,0:T(8,128)(2,1)}) %all-gather.8.cloned.1.call-update) | async-done | bytes 4194320 | tf_op jit(solution)/shard_map/all_gather | solution.py:45
  107.4 53.3 %all-gather.10.cloned.1.call-done = bf16[4096,640]{1,0:T(8,128)(2,1)} async-done(((bf16[128,640]{1,0:T(8,128)(2,1)}), bf16[4096,640]{1,0:T(8,128)(2,1)}) %all-gather.10.cloned.1.call-update) | async-done | bytes 5242896 | tf_op jit(solution)/shard_map/all_gather | solution.py:47
  160.7 8.2 %fusion.21 = bf16[512,640]{1,0:T(8,128)(2,1)} fusion(bf16[512,4096]{1,0:T(8,128)(2,1)} %all-gather.8.cloned.1.call-done, bf16[4096,640]{1,0:T(8,128)(2,1)} %all-gather.10.cloned.1.call-done, f32[640]{0:T(1024)S(1)} %convert_element_type.24), kind=kOutput, calls=%fused_computation.26 | convolution fusion | flops 2687631360 | bytes 10095104 | tf_op jit(solution)/shard_map/dot_general | solution.py:23
  169.0 0.0 all-gather.14.cloned.1.call-start
  169.0 0.5 all-gather.14.cloned.1.call-update
  169.6 43.9 %all-gather.18.cloned.1.call-done = bf16[5120,384]{1,0:T(8,128)(2,1)} async-done(((bf16[160,384]{1,0:T(8,128)(2,1)}), bf16[5120,384]{1,0:T(8,128)(2,1)}) %all-gather.18.cloned.1.call-update) | async-done | bytes 3932176 | tf_op jit(solution)/shard_map/all_gather | solution.py:56
  213.5 66.1 %all-gather.12.cloned.1.call-done = bf16[512,5120]{1,0:T(8,128)(2,1)} async-done(((bf16[512,640]{1,0:T(8,128)(2,1)}), bf16[512,5120]{1,0:T(8,128)(2,1)}) %all-gather.12.cloned.1.call-update) | async-done | bytes 5242896 | tf_op jit(solution)/shard_map/all_gather | solution.py:51
  279.6 7.3 %convolution_convert_fusion = bf16[512,384]{1,0:T(8,128)(2,1)} fusion(bf16[512,5120]{1,0:T(8,128)(2,1)} %all-gather.12.cloned.1.call-done, bf16[5120,384]{1,0:T(8,128)(2,1)} %all-gather.18.cloned.1.call-done), kind=kOutput, calls=%fused_computation.29 | convolution fusion | flops 2013462528 | bytes 9568256 | tf_op jit(solution)/shard_map/dot_general | solution.py:23
  286.9 0.2 all-gather.16.cloned.1.call-start
  287.2 43.9 %all-gather.14.cloned.1.call-done = bf16[5120,384]{1,0:T(8,128)(2,1)} async-done(((bf16[160,384]{1,0:T(8,128)(2,1)}), bf16[5120,384]{1,0:T(8,128)(2,1)}) %all-gather.14.cloned.1.call-update) | async-done | bytes 3932176 | tf_op jit(solution)/shard_map/all_gather | solution.py:57
  331.1 7.3 %fusion.22 = bf16[512,384]{1,0:T(8,128)(2,1)} fusion(bf16[512,5120]{1,0:T(8,128)(2,1)} %all-gather.12.cloned.1.call-done, bf16[5120,384]{1,0:T(8,128)(2,1)} %all-gather.14.cloned.1.call-done, f32[384]{0:T(512)S(1)} %convert_element_type.26), kind=kOutput, calls=%fused_computation.28 | convolution fusion | flops 2013659136 | bytes 9569792 | tf_op jit(solution)/shard_map/dot_general | solution.py:23
  338.5 0.3 copy.30
  338.8 0.6 dynamic_slice.3
  339.4 0.6 iota_compare_fusion
  340.0 38.0 %all-gather.20.cloned.1.call-done = bf16[512,3072]{1,0:T(8,128)(2,1)} async-done(((bf16[512,384]{1,0:T(8,128)(2,1)}), bf16[512,3072]{1,0:T(8,128)(2,1)}) %all-gather.20.cloned.1.call-update) | async-done | bytes 3145744 | tf_op jit(solution)/shard_map/all_gather | solution.py:64
  378.0 3.7 fusion.9
  381.7 9.1 %fusion.30 = (f32[24,256]{1,0:T(8,128)S(1)}, f32[24,256,512]{1,2,0:T(8,128)}) fusion(f32[24,512,256]{2,1,0:T(8,128)S(1)} %fusion.9, pred[512]{0:T(512)(128)(4,1)S(1)} %iota_compare_fusion), kind=kOutput, calls=%fused_computation.45 | output fusion | flops 18874880 | bytes 25190912 | tf_op jit(solution)/shard_map/sub | solution.py:16
  390.7 33.1 %all-gather.16.cloned.1.call-done = bf16[512,3072]{1,0:T(8,128)(2,1)} async-done(((bf16[512,384]{1,0:T(8,128)(2,1)}), bf16[512,3072]{1,0:T(8,128)(2,1)}) %all-gather.16.cloned.1.call-update) | async-done | bytes 3145744 | tf_op jit(solution)/shard_map/all_gather | solution.py:65
  423.9 3.2 copy.28
  427.1 6.8 %fusion.12 = bf16[24,128,256]{2,1,0:T(8,128)(2,1)} fusion(bf16[512,24,128]{0,2,1:T(8,128)(2,1)S(1)} %bitcast.36, f32[24,256,512]{1,2,0:T(8,128)} %get-tuple-element.6, f32[24,256]{1,0:T(8,128)S(1)} %get-tuple-element.5), kind=kOutput, calls=%fused_computation.16 | convolution fusion | flops 812384256 | bytes 17326080 | tf_op jit(solution)/shard_map/hrk,khd->rhd/dot_general | solution.py:18
  433.9 2.6 copy.26
  (20 shorter events, 0.2 us)
Async XLA Ops:
  6.5 12.1 %copy-start.3 = (s32[32]{0:T(128)S(1)}, s32[32]{0:T(128)}, u32[]{:S(2)}) copy-start(s32[32]{0:T(128)} %param.10) | copy-start | bytes 388
  8.9 44.2 %copy-start.1 = (bf16[640]{0:T(1024)(128)(2,1)S(1)}, bf16[640]{0:T(1024)(128)(2,1)}, u32[]{:S(2)}) copy-start(bf16[640]{0:T(1024)(128)(2,1)} %param.14) | copy-start | bytes 3844
  10.9 22.1 %all-to-all-start = ((bf16[2,32,2,4096]{3,2,0,1:T(2,128)(2,1)}), bf16[2,32,2,4096]{3,2,0,1:T(2,128)(2,1)S(1)}, u32[]{:S(2)}, u32[]{:S(2)}) async-start(bf16[2,32,2,4096]{3,2,0,1:T(2,128)(2,1)} %copy.21), calls=%async_computation | async-start | bytes 2097152 | tf_op jit(solution)/shard_map/all_to_all | solution.py:32
  18.6 88.9 %all-gather.8.cloned.1.call-start = ((), (), s32[]{:S(2)}) async-start(), calls=%async_computation.2 | async-start | bytes 4718592 | tf_op jit(solution)/shard_map/all_gather | solution.py:45
  51.6 109.1 %all-gather.10.cloned.1.call-start = ((), (), s32[]{:S(2)}) async-start(), calls=%async_computation.3 | async-start | bytes 5406720 | tf_op jit(solution)/shard_map/all_gather | solution.py:47
  52.3 161.2 %all-gather.18.cloned.1.call-start = ((), (), s32[]{:S(2)}) async-start(), calls=%async_computation.7 | async-start | bytes 4055040 | tf_op jit(solution)/shard_map/all_gather | solution.py:56
  53.1 226.6 %all-gather.12.cloned.1.call-start = ((), (), s32[]{:S(2)}) async-start(), calls=%async_computation.4 | async-start | bytes 5898240 | tf_op jit(solution)/shard_map/all_gather | solution.py:51
  169.0 162.1 %all-gather.14.cloned.1.call-start = ((), (), s32[]{:S(2)}) async-start(), calls=%async_computation.5 | async-start | bytes 4055040 | tf_op jit(solution)/shard_map/all_gather | solution.py:57
  169.6 117.6 %copy-start.2 = (bf16[384]{0:T(512)(128)(2,1)S(1)}, bf16[384]{0:T(512)(128)(2,1)}, u32[]{:S(2)}) copy-start(bf16[384]{0:T(512)(128)(2,1)} %param.17) | copy-start | bytes 2308
  169.6 208.4 %all-gather.20.cloned.1.call-start = ((), (), s32[]{:S(2)}) async-start(), calls=%async_computation.8 | async-start | bytes 3538944 | tf_op jit(solution)/shard_map/all_gather | solution.py:64
  286.9 136.9 %all-gather.16.cloned.1.call-start = ((), (), s32[]{:S(2)}) async-start(), calls=%async_computation.6 | async-start | bytes 3538944 | tf_op jit(solution)/shard_map/all_gather | solution.py:65
  287.2 51.3 %copy-start = (bf16[1,256,3072]{2,1,0:T(8,128)(2,1)S(1)}, bf16[1,256,3072]{2,1,0:T(8,128)(2,1)}, u32[]{:S(2)}) copy-start(bf16[1,256,3072]{2,1,0:T(8,128)(2,1)} %param.12) | copy-start | bytes 4718596
  287.2 51.6 %copy-start.4 = (s32[32]{0:T(128)S(1)}, s32[32]{0:T(128)}, u32[]{:S(2)}) copy-start(s32[32]{0:T(128)} %param.11) | copy-start | bytes 388
Sparse Core Ops, SparseCore 0:
  51.7 55.6 all-gather.7
  110.0 50.7 all-gather.9
  163.3 50.2 all-gather.17
  215.2 64.3 all-gather.11
  282.0 49.0 all-gather.13
  332.7 45.2 all-gather.19
  379.8 44.0 all-gather.15
where the time goes:
time: 444 us; the launch traced here: 443 us
  waiting for transfers between devices  349 us (79%)
  matrix products  33.4 us (8%)
  blocking collectives  15.9 us (4%)
  local copies, waits for them, and re-layouts  13.7 us (3%)
  between operations  13.6 us (3%)
  other arithmetic  9.71 us (2%)
  starting transfers between devices  8.08 us (2%)
    all_gather x1, waiting for transfers between devices, body(): hidden = lax.all_gather(hidden_part, 'seq', axis=1, tiled=True)  66.1 us
    all_gather x1, waiting for transfers between devices, body(): text_rows = lax.all_gather(arrived, 'seq', axis=0, tiled=True)  54.3 us
    all_gather x1, waiting for transfers between devices, body(): lax.all_gather(w_text, 'job', axis=0, tiled=True)  53.3 us
    all_gather x1, waiting for transfers between devices, body(): key_sums = single_step(lax.all_gather(w_key, 'job', axis=0, tiled=True))  43.9 us
    all_gather x1, waiting for transfers between devices, body(): value_sums = single_step(lax.all_gather(w_value, 'job', axis=0, tiled=True))  43.9 us
    all_gather x1, waiting for transfers between devices, body(): lax.all_gather(keys, 'seq', axis=1, tiled=True)  38 us
    all_gather x1, waiting for transfers between devices, body(): lax.all_gather(values, 'seq', axis=1, tiled=True)  33.1 us
    dot_general x3, matrix products, add_product(): return jnp.dot(left, portion, preferred_element_type=jnp.float32)  22.9 us
  transfers between devices with their start and end apart: 8, of which 8 were waited for; matrix products, arithmetic and copies ran while one was open for 8% of the time, Pallas kernels for 0%

commit v1 on v0

--- a/solution.py
+++ b/solution.py
@@ -42,7 +42,12 @@
     arrived = lax.all_to_all(picked, "job", split_axis=0, concat_axis=0, tiled=True).reshape(
         rows_local, text_width
     )
-    text_rows = lax.all_gather(arrived, "seq", axis=0, tiled=True)
+    ring = [arrived]
+    for hop in range(7):
+        ring.append(lax.ppermute(ring[-1], "seq", [(dev, (dev + 1) % 8) for dev in range(8)]))
+    text_rows = jnp.roll(
+        jnp.concatenate(ring[::-1], axis=0), (lax.axis_index("seq") + 1) * ring[0].shape[0], axis=0
+    )
     text_count = text_rows.shape[0]
     preact = add_product(text_rows, lax.all_gather(w_text, "job", axis=0, tiled=True))
     hidden_part = jax.nn.gelu(preact + b_text.astype(jnp.float32), approximate=True).astype(

time: 444 us -> 417 us (0.939)
  waiting for transfers between devices: 349 us -> 303 us
  local copies, waits for them, and re-layouts: 13.7 us -> 30.5 us
    ppermute x0 -> x7, waiting for transfers between devices: none -> 95 us  [body(): lax.ppermute(ring[-1], 'seq', [(dev, (dev + 1) % 8) for dev in range(8)])]
    all_gather x1 -> x0, waiting for transfers between devices: 54.3 us -> none  [body(): text_rows = lax.all_gather(arrived, 'seq', axis=0, tiled=True)]
    all_gather x1, waiting for transfers between devices: 53.3 us -> 0.01 us  [body(): lax.all_gather(w_text, 'job', axis=0, tiled=True)]
    all_gather x1, waiting for transfers between devices: 43.9 us -> 10 us  [body(): key_sums = single_step(lax.all_gather(w_key, 'job', axis=0, tiled=True))]
    unnamed x12 -> x25, local copies, waits for them, and re-layouts: 2.66 us -> 19.3 us
  transfers between devices with their start and end apart: 8 -> 14, of which waited for: 8 -> 13; matrix products, arithmetic and copies ran while one was open for 8% -> 15% of each run, Pallas kernels for 0% -> 0%
where the time goes in v1:
time: 417 us
  waiting for transfers between devices  303 us (73%)
  matrix products  33.4 us (8%)
  local copies, waits for them, and re-layouts  30.5 us (7%)
  blocking collectives  16.2 us (4%)
  between operations  13.6 us (3%)
  other arithmetic  10.3 us (2%)
  starting transfers between devices  10.2 us (2%)
    ppermute x7, waiting for transfers between devices, body(): lax.ppermute(ring[-1], 'seq', [(dev, (dev + 1) % 8) for dev in range(8)])  95 us
    all_gather x1, waiting for transfers between devices, body(): hidden = lax.all_gather(hidden_part, 'seq', axis=1, tiled=True)  66.2 us
    all_gather x1, waiting for transfers between devices, body(): value_sums = single_step(lax.all_gather(w_value, 'job', axis=0, tiled=True))  44.1 us
    all_gather x1, waiting for transfers between devices, body(): lax.all_gather(keys, 'seq', axis=1, tiled=True)  38.1 us
    all_gather x1, waiting for transfers between devices, body(): lax.all_gather(values, 'seq', axis=1, tiled=True)  33 us
    dot_general x3, matrix products, add_product(): return jnp.dot(left, portion, preferred_element_type=jnp.float32)  22.9 us
    unnamed x25, local copies, waits for them, and re-layouts  19.3 us
    all_to_all x1, blocking collectives, body(): lax.all_to_all(picked, 'job', split_axis=0, concat_axis=0, tiled=True)  16.2 us
  transfers between devices with their start and end apart: 14, of which 13 were waited for; matrix products, arithmetic and copies ran while one was open for 15% of the time, Pallas kernels for 0%

profile of v1, /device:TPU:2, one launch (start us, length us, event | category | flops | bytes accessed | tf_op | source)
XLA Modules:
  0.0 416.7 jit_solution(7824148042231651657)
XLA Ops:
  7.3 2.3 copy.20
  9.6 2.1 copy.21
  11.6 7.6 %all-to-all-start = ((bf16[2,32,2,4096]{3,2,0,1:T(2,128)(2,1)}), bf16[2,32,2,4096]{3,2,0,1:T(2,128)(2,1)S(1)}, u32[]{:S(2)}, u32[]{:S(2)}) async-start(bf16[2,32,2,4096]{3,2,0,1:T(2,128)(2,1)} %copy.21), calls=%async_computation | async-start | bytes 2097152 | tf_op jit(solution)/shard_map/all_to_all | solution.py:32
  20.0 14.9 %all-to-all-done = bf16[2,32,2,4096]{3,2,0,1:T(2,128)(2,1)S(1)} async-done(((bf16[2,32,2,4096]{3,2,0,1:T(2,128)(2,1)}), bf16[2,32,2,4096]{3,2,0,1:T(2,128)(2,1)S(1)}, u32[]{:S(2)}, u32[]{:S(2)}) %all-to-all-start) | async-done | bytes 1048608 | tf_op jit(solution)/shard_map/all_to_all | solution.py:32
  34.9 1.6 gather_fusion
  36.6 16.2 %all_to_all.10 = bf16[32,2,4096]{2,1,0:T(2,128)(2,1)S(1)} all-to-all(bf16[32,2,4096]{2,1,0:T(2,128)(2,1)S(1)} %gather_fusion), channel_id=1, replica_groups=mesh['job'=32,'seq'=8] {'job'}, dimensions={0} | all-to-all | bytes 1048576 | tf_op jit(solution)/shard_map/all_to_all | solution.py:42
  52.9 2.2 collective-permute-start
  55.1 17.0 %collective-permute-done = bf16[64,4096]{1,0:T(8,128)(2,1)S(1)} collective-permute-done((bf16[64,4096]{1,0:T(8,128)(2,1)S(1)}, bf16[64,4096]{1,0:T(8,128)(2,1)S(1)}, u32[]{:S(2)}, u32[]{:S(2)}) %collective-permute-start) | collective-permute-done | bytes 524320 | tf_op jit(solution)/shard_map/ppermute | solution.py:47
  72.2 15.2 %collective-permute-done.1 = bf16[64,4096]{1,0:T(8,128)(2,1)S(1)} collective-permute-done((bf16[64,4096]{1,0:T(8,128)(2,1)S(1)}, bf16[64,4096]{1,0:T(8,128)(2,1)S(1)}, u32[]{:S(2)}, u32[]{:S(2)}) %collective-permute-start.1) | collective-permute-done | bytes 524320 | tf_op jit(solution)/shard_map/ppermute | solution.py:47
  87.3 14.3 %collective-permute-done.2 = bf16[64,4096]{1,0:T(8,128)(2,1)S(1)} collective-permute-done((bf16[64,4096]{1,0:T(8,128)(2,1)S(1)}, bf16[64,4096]{1,0:T(8,128)(2,1)S(1)}, u32[]{:S(2)}, u32[]{:S(2)}) %collective-permute-start.2) | collective-permute-done | bytes 524320 | tf_op jit(solution)/shard_map/ppermute | solution.py:47
  101.6 13.4 %collective-permute-done.3 = bf16[64,4096]{1,0:T(8,128)(2,1)S(1)} collective-permute-done((bf16[64,4096]{1,0:T(8,128)(2,1)S(1)}, bf16[64,4096]{1,0:T(8,128)(2,1)S(1)}, u32[]{:S(2)}, u32[]{:S(2)}) %collective-permute-start.3) | collective-permute-done | bytes 524320 | tf_op jit(solution)/shard_map/ppermute | solution.py:47
  115.0 12.5 %collective-permute-done.4 = bf16[64,4096]{1,0:T(8,128)(2,1)S(1)} collective-permute-done((bf16[64,4096]{1,0:T(8,128)(2,1)S(1)}, bf16[64,4096]{1,0:T(8,128)(2,1)S(1)}, u32[]{:S(2)}, u32[]{:S(2)}) %collective-permute-start.4) | collective-permute-done | bytes 524320 | tf_op jit(solution)/shard_map/ppermute | solution.py:47
  127.5 11.9 %collective-permute-done.5 = bf16[64,4096]{1,0:T(8,128)(2,1)} collective-permute-done((bf16[64,4096]{1,0:T(8,128)(2,1)S(1)}, bf16[64,4096]{1,0:T(8,128)(2,1)}, u32[]{:S(2)}, u32[]{:S(2)}) %collective-permute-start.5) | collective-permute-done | bytes 524320 | tf_op jit(solution)/shard_map/ppermute | solution.py:47
  139.7 10.7 %collective-permute-done.6 = bf16[64,4096]{1,0:T(8,128)(2,1)} collective-permute-done((bf16[64,4096]{1,0:T(8,128)(2,1)}, bf16[64,4096]{1,0:T(8,128)(2,1)}, u32[]{:S(2)}, u32[]{:S(2)}) %collective-permute-start.6) | collective-permute-done | bytes 524320 | tf_op jit(solution)/shard_map/ppermute | solution.py:47
  150.4 1.9 constant_dynamic-update-slice_fusion.15
  152.3 1.9 constant_dynamic-update-slice_fusion.14
  159.2 1.9 constant_dynamic-update-slice_fusion.7
  161.0 1.9 constant_dynamic-update-slice_fusion.6
  167.1 0.9 constant_dynamic-update-slice_fusion
  168.0 8.2 %fusion.26 = bf16[512,640]{1,0:T(8,128)(2,1)} fusion(bf16[4096,640]{1,0:T(8,128)(2,1)} %all-gather.7.cloned.1.call-done, bf16[1024,4096]{1,0:T(8,128)(2,1)} %constant_dynamic-update-slice_fusion, s32[]{:T(128)S(6)} %select_n.45, f32[640]{0:T(1024)S(1)} %convert_element_type.24), kind=kOutput, calls=%fused_computation.28 | convolution fusion | flops 2687631360 | bytes 10095108 | tf_op jit(solution)/shard_map/dot_general | solution.py:23
  176.9 10.0 %all-gather.15.cloned.1.call-done = bf16[5120,384]{1,0:T(8,128)(2,1)} async-done(((bf16[160,384]{1,0:T(8,128)(2,1)}), bf16[5120,384]{1,0:T(8,128)(2,1)}) %all-gather.15.cloned.1.call-update) | async-done | bytes 3932176 | tf_op jit(solution)/shard_map/all_gather | solution.py:61
  186.9 66.2 %all-gather.9.cloned.1.call-done = bf16[512,5120]{1,0:T(8,128)(2,1)} async-done(((bf16[512,640]{1,0:T(8,128)(2,1)}), bf16[512,5120]{1,0:T(8,128)(2,1)}) %all-gather.9.cloned.1.call-update) | async-done | bytes 5242896 | tf_op jit(solution)/shard_map/all_gather | solution.py:56
  253.2 7.3 %convolution_convert_fusion = bf16[512,384]{1,0:T(8,128)(2,1)} fusion(bf16[512,5120]{1,0:T(8,128)(2,1)} %all-gather.9.cloned.1.call-done, bf16[5120,384]{1,0:T(8,128)(2,1)} %all-gather.15.cloned.1.call-done), kind=kOutput, calls=%fused_computation.31 | convolution fusion | flops 2013462528 | bytes 9568256 | tf_op jit(solution)/shard_map/dot_general | solution.py:23
  260.6 44.1 %all-gather.11.cloned.1.call-done = bf16[5120,384]{1,0:T(8,128)(2,1)} async-done(((bf16[160,384]{1,0:T(8,128)(2,1)}), bf16[5120,384]{1,0:T(8,128)(2,1)}) %all-gather.11.cloned.1.call-update) | async-done | bytes 3932176 | tf_op jit(solution)/shard_map/all_gather | solution.py:62
  304.7 7.3 %fusion.29 = bf16[512,384]{1,0:T(8,128)(2,1)} fusion(bf16[512,5120]{1,0:T(8,128)(2,1)} %all-gather.9.cloned.1.call-done, bf16[5120,384]{1,0:T(8,128)(2,1)} %all-gather.11.cloned.1.call-done, f32[384]{0:T(512)S(1)} %convert_element_type.26), kind=kOutput, calls=%fused_computation.30 | convolution fusion | flops 2013659136 | bytes 9569792 | tf_op jit(solution)/shard_map/dot_general | solution.py:23
  313.5 38.1 %all-gather.17.cloned.1.call-done = bf16[512,3072]{1,0:T(8,128)(2,1)} async-done(((bf16[512,384]{1,0:T(8,128)(2,1)}), bf16[512,3072]{1,0:T(8,128)(2,1)}) %all-gather.17.cloned.1.call-update) | async-done | bytes 3145744 | tf_op jit(solution)/shard_map/all_gather | solution.py:69
  351.6 3.7 fusion.11
  355.2 9.0 %fusion.38 = (f32[24,256]{1,0:T(8,128)S(1)}, f32[24,256,512]{1,2,0:T(8,128)}) fusion(f32[24,512,256]{2,1,0:T(8,128)S(1)} %fusion.11, pred[512]{0:T(512)(128)(4,1)S(1)} %iota_compare_fusion), kind=kOutput, calls=%fused_computation.64 | output fusion | flops 18874880 | bytes 25190912 | tf_op jit(solution)/shard_map/sub | solution.py:16
  364.3 33.0 %all-gather.13.cloned.1.call-done = bf16[512,3072]{1,0:T(8,128)(2,1)} async-done(((bf16[512,384]{1,0:T(8,128)(2,1)}), bf16[512,3072]{1,0:T(8,128)(2,1)}) %all-gather.13.cloned.1.call-update) | async-done | bytes 3145744 | tf_op jit(solution)/shard_map/all_gather | solution.py:70
  397.3 3.2 copy.28
  400.5 6.8 %fusion.14 = bf16[24,128,256]{2,1,0:T(8,128)(2,1)} fusion(bf16[512,24,128]{0,2,1:T(8,128)(2,1)S(1)} %bitcast.35, f32[24,256,512]{1,2,0:T(8,128)} %get-tuple-element.6, f32[24,256]{1,0:T(8,128)S(1)} %get-tuple-element.5), kind=kOutput, calls=%fused_computation.18 | convolution fusion | flops 812384256 | bytes 17326080 | tf_op jit(solution)/shard_map/hrk,khd->rhd/dot_general | solution.py:18
  407.3 2.6 copy.26
  (45 shorter events, 13.2 us)
Async XLA Ops:
  6.5 133.1 %copy-start.1 = (bf16[640]{0:T(1024)(128)(2,1)S(1)}, bf16[640]{0:T(1024)(128)(2,1)}, u32[]{:S(2)}) copy-start(bf16[640]{0:T(1024)(128)(2,1)} %param.14) | copy-start | bytes 3844
  6.5 161.5 %all-gather.7.cloned.1.call-start = ((), (), s32[]{:S(2)}) async-start(), calls=%async_computation.2 | async-start | bytes 5406720 | tf_op jit(solution)/shard_map/all_gather | solution.py:52
  11.6 23.3 %all-to-all-start = ((bf16[2,32,2,4096]{3,2,0,1:T(2,128)(2,1)}), bf16[2,32,2,4096]{3,2,0,1:T(2,128)(2,1)S(1)}, u32[]{:S(2)}, u32[]{:S(2)}) async-start(bf16[2,32,2,4096]{3,2,0,1:T(2,128)(2,1)} %copy.21), calls=%async_computation | async-start | bytes 2097152 | tf_op jit(solution)/shard_map/all_to_all | solution.py:32
  19.3 167.6 %all-gather.15.cloned.1.call-start = ((), (), s32[]{:S(2)}) async-start(), calls=%async_computation.6 | async-start | bytes 4055040 | tf_op jit(solution)/shard_map/all_gather | solution.py:61
  52.9 19.2 %collective-permute-start = (bf16[64,4096]{1,0:T(8,128)(2,1)S(1)}, bf16[64,4096]{1,0:T(8,128)(2,1)S(1)}, u32[]{:S(2)}, u32[]{:S(2)}) collective-permute-start(bf16[64,4096]{1,0:T(8,128)(2,1)S(1)} %reshape.17), channel_id=1, source_target_pairs={{0,1},{1,2},{2,3},{3,4},{4,5},{5,6},{6,7},{7,0},{8,9},{9,10},{10,1... | collective-permute-start | bytes 1572872 | tf_op jit(solution)/shard_map/ppermute | solution.py:47
  72.1 15.2 %collective-permute-start.1 = (bf16[64,4096]{1,0:T(8,128)(2,1)S(1)}, bf16[64,4096]{1,0:T(8,128)(2,1)S(1)}, u32[]{:S(2)}, u32[]{:S(2)}) collective-permute-start(bf16[64,4096]{1,0:T(8,128)(2,1)S(1)} %collective-permute-done), channel_id=1, source_target_pairs={{0,1},{1,2},{2,3},{3,4},{4,5},{5,6},{6,7},{7,0},{8,9},{9,10},{10,1... | collective-permute-start | bytes 1572872 | tf_op jit(solution)/shard_map/ppermute | solution.py:47
  87.3 14.3 %collective-permute-start.2 = (bf16[64,4096]{1,0:T(8,128)(2,1)S(1)}, bf16[64,4096]{1,0:T(8,128)(2,1)S(1)}, u32[]{:S(2)}, u32[]{:S(2)}) collective-permute-start(bf16[64,4096]{1,0:T(8,128)(2,1)S(1)} %collective-permute-done.1), channel_id=1, source_target_pairs={{0,1},{1,2},{2,3},{3,4},{4,5},{5,6},{6,7},{7,0},{8,9},{9,10},{10,1... | collective-permute-start | bytes 1572872 | tf_op jit(solution)/shard_map/ppermute | solution.py:47
  101.6 13.4 %collective-permute-start.3 = (bf16[64,4096]{1,0:T(8,128)(2,1)S(1)}, bf16[64,4096]{1,0:T(8,128)(2,1)S(1)}, u32[]{:S(2)}, u32[]{:S(2)}) collective-permute-start(bf16[64,4096]{1,0:T(8,128)(2,1)S(1)} %collective-permute-done.2), channel_id=1, source_target_pairs={{0,1},{1,2},{2,3},{3,4},{4,5},{5,6},{6,7},{7,0},{8,9},{9,10},{10,1... | collective-permute-start | bytes 1572872 | tf_op jit(solution)/shard_map/ppermute | solution.py:47
  115.0 12.5 %collective-permute-start.4 = (bf16[64,4096]{1,0:T(8,128)(2,1)S(1)}, bf16[64,4096]{1,0:T(8,128)(2,1)S(1)}, u32[]{:S(2)}, u32[]{:S(2)}) collective-permute-start(bf16[64,4096]{1,0:T(8,128)(2,1)S(1)} %collective-permute-done.3), channel_id=1, source_target_pairs={{0,1},{1,2},{2,3},{3,4},{4,5},{5,6},{6,7},{7,0},{8,9},{9,10},{10,1... | collective-permute-start | bytes 1572872 | tf_op jit(solution)/shard_map/ppermute | solution.py:47
  127.5 11.9 %collective-permute-start.5 = (bf16[64,4096]{1,0:T(8,128)(2,1)S(1)}, bf16[64,4096]{1,0:T(8,128)(2,1)}, u32[]{:S(2)}, u32[]{:S(2)}) collective-permute-start(bf16[64,4096]{1,0:T(8,128)(2,1)S(1)} %collective-permute-done.4), channel_id=1, source_target_pairs={{0,1},{1,2},{2,3},{3,4},{4,5},{5,6},{6,7},{7,0},{8,9},{9,10},{10,1... | collective-permute-start | bytes 1572872 | tf_op jit(solution)/shard_map/ppermute | solution.py:47
  139.4 11.0 %collective-permute-start.6 = (bf16[64,4096]{1,0:T(8,128)(2,1)}, bf16[64,4096]{1,0:T(8,128)(2,1)}, u32[]{:S(2)}, u32[]{:S(2)}) collective-permute-start(bf16[64,4096]{1,0:T(8,128)(2,1)} %collective-permute-done.5), channel_id=1, source_target_pairs={{0,1},{1,2},{2,3},{3,4},{4,5},{5,6},{6,7},{7,0},{8,9},{9,10},{10,1... | collective-permute-start | bytes 1572872 | tf_op jit(solution)/shard_map/ppermute | solution.py:47
  139.4 113.8 %all-gather.9.cloned.1.call-start = ((), (), s32[]{:S(2)}) async-start(), calls=%async_computation.3 | async-start | bytes 5898240 | tf_op jit(solution)/shard_map/all_gather | solution.py:56
  176.3 128.4 %all-gather.11.cloned.1.call-start = ((), (), s32[]{:S(2)}) async-start(), calls=%async_computation.4 | async-start | bytes 4055040 | tf_op jit(solution)/shard_map/all_gather | solution.py:62
  176.8 83.7 %copy-start.2 = (bf16[384]{0:T(512)(128)(2,1)S(1)}, bf16[384]{0:T(512)(128)(2,1)}, u32[]{:S(2)}) copy-start(bf16[384]{0:T(512)(128)(2,1)} %param.17) | copy-start | bytes 2308
  176.9 174.7 %all-gather.17.cloned.1.call-start = ((), (), s32[]{:S(2)}) async-start(), calls=%async_computation.7 | async-start | bytes 3538944 | tf_op jit(solution)/shard_map/all_gather | solution.py:69
  260.5 136.8 %all-gather.13.cloned.1.call-start = ((), (), s32[]{:S(2)}) async-start(), calls=%async_computation.5 | async-start | bytes 3538944 | tf_op jit(solution)/shard_map/all_gather | solution.py:70
  260.6 51.4 %copy-start = (bf16[1,256,3072]{2,1,0:T(8,128)(2,1)S(1)}, bf16[1,256,3072]{2,1,0:T(8,128)(2,1)}, u32[]{:S(2)}) copy-start(bf16[1,256,3072]{2,1,0:T(8,128)(2,1)} %param.12) | copy-start | bytes 4718596
  260.6 51.8 %copy-start.3 = (s32[32]{0:T(128)S(1)}, s32[32]{0:T(128)}, u32[]{:S(2)}) copy-start(s32[32]{0:T(128)} %param.11) | copy-start | bytes 388
Sparse Core Ops, SparseCore 0:
  9.9 58.9 all-gather.6
  139.5 47.3 all-gather.14
  188.7 64.3 all-gather.8
  255.6 49.0 all-gather.10
  306.3 45.2 all-gather.16
  353.2 44.0 all-gather.12
